TPU v7x, 256 devices: a whole 4x4x8 slice. The times are simulated.
256 devices in a mesh: pipe: 4 (over x), seq: 32 (over z, y), batch: 2 (over core).
Axes of the slice: x: 4, y: 4, z: 8, core: 2. Of those that a mesh axis runs over, the one named last changes fastest.
Arguments:
- latent_noise: float32 [4, 2, 512, 64], P('pipe', 'batch', 'seq'), may hold values from -6 to 6
- text_rows: bfloat16 [4, 2, 256, 4096], P(None, 'batch', None, 'seq'), may hold values from -6 to 6
- text_lengths: int32 [4, 2], P(None, 'batch'), may hold values from 32 to 256, as said below
- plan: int32 [3], replicated, may hold values from 1 to 1000, as said below
- context_weight: bfloat16 [4096, 1536], P('seq'), may hold values from -0.09375 to 0.09375
- w_embed: bfloat16 [64, 1536], replicated, may hold values from -0.75 to 0.75
- w_attention: bfloat16 [4, 1536, 4608], P('pipe', 'batch'), may hold values from -1 to 1
- w_project: bfloat16 [4, 1536, 1536], P('pipe', 'batch'), may hold values from -0.15625 to 0.15625
- w_modulate: bfloat16 [4, 256, 4608], P('pipe', 'batch'), may hold values from -0.375 to 0.375
- w_final: bfloat16 [1536, 64], replicated, may hold values from -0.15625 to 0.15625
Outputs:
- final_latent: float32 [4, 2, 512, 64], P('pipe', 'batch', 'seq')
Inputs may be any that keep to these rules, and one draw needn't show every extreme that they name: `text_lengths`: at least one prompt has 256 live rows and one has 32. `plan`: strictly falling; the first entry is 1000 and the last is 1.
All inputs are finite; a program needn't handle non-finite values.
Results may differ from a plain program's by a relative error of at most 0.02.
Values may be sent and summed in bfloat16 or wider, within the bound.
No kernel may reach another device: no remote copies, remote signals or barrier semaphores. Data moves between devices by JAX's collectives and lax.ppermute only.
A program may use at most 128 MiB of HBM per device.

v0:
```python
import math
import jax
import jax.numpy as jnp
from jax import lax
from jax.sharding import PartitionSpec as P

HEADS = 16
STEPS = 2
epsilon = 1e-06


def shifted(value, axis, by):
    peers = lax.axis_size(axis)
    return lax.ppermute(value, axis, [(i, (i + by) % peers) for i in range(peers)])


def layer_norm(hidden):
    values = hidden.astype(jnp.float32)
    center = values - jnp.mean(values, axis=-1, keepdims=True)
    spread = jnp.mean(center * center, axis=-1, keepdims=True)
    return center * lax.rsqrt(spread + epsilon)


def time_features(noise_level, feature_count):
    half_count = feature_count // 2
    wave_frequency = jnp.exp(
        -math.log(10000.0) * jnp.arange(half_count, dtype=jnp.float32) / half_count
    )
    angles = noise_level * wave_frequency
    return jnp.concatenate([jnp.cos(angles), jnp.sin(angles)]).astype(jnp.bfloat16)


def on_device(
    latent_noise,
    text_rows,
    text_lengths,
    plan,
    context_weight,
    w_embed,
    w_attention,
    w_project,
    w_modulate,
    w_final,
):
    seq_count = lax.axis_size("seq")
    device_count = lax.axis_size("pipe")
    section = lax.axis_index("pipe")
    tokens_here = latent_noise.shape[2]
    text_total = text_rows.shape[2]
    text_here = text_total // seq_count
    model_width = w_embed.shape[1]
    gathered = (
        lax.all_gather(w_attention, "batch", axis=1, tiled=True),
        lax.all_gather(w_project, "batch", axis=1, tiled=True),
        lax.all_gather(w_modulate, "batch", axis=1, tiled=True),
    )
    attn_weight = gathered[0][0]
    proj_weight = gathered[1][0]
    mod_weight = gathered[2][0]
    inner_width = proj_weight.shape[0]
    head_size = inner_width // HEADS
    unit_count = max(HEADS, seq_count)
    replica_count = unit_count // HEADS
    unit_here = unit_count // seq_count
    query_rows = tokens_here // replica_count
    factor = 1.0 / math.sqrt(head_size)
    resident_text = text_rows[:, 0]
    context = lax.psum_scatter(
        jnp.einsum(
            "ipe,ea->pia", resident_text, context_weight, preferred_element_type=jnp.float32
        ),
        "seq",
        scatter_dimension=0,
        tiled=True,
    ).astype(jnp.bfloat16)
    live_text = jnp.arange(text_total)[None, :] < text_lengths[:, 0][:, None]

    def key_units(key_rows):
        row_count = key_rows.shape[0]
        heads_first = key_rows.reshape(row_count, HEADS, head_size).transpose(1, 0, 2)
        return jnp.repeat(heads_first, replica_count, axis=0).reshape(
            unit_count, row_count * head_size
        )

    def query_units(query_block):
        parted = query_block.reshape(replica_count, query_rows, HEADS, head_size).transpose(
            2, 0, 1, 3
        )
        return parted.reshape(unit_count, query_rows * head_size)

    def from_units(blocks):
        parted = blocks.reshape(HEADS, replica_count, query_rows, head_size).transpose(1, 2, 0, 3)
        return parted.reshape(tokens_here, inner_width)

    def split_joined(moved):
        parted = moved.reshape(unit_here, seq_count, tokens_here + text_here, head_size)
        image_part = parted[:, :, :tokens_here].reshape(
            unit_here, seq_count * tokens_here, head_size
        )
        text_part = parted[:, :, tokens_here:].reshape(unit_here, seq_count * text_here, head_size)
        return jnp.concatenate([image_part, text_part], 1)

    text_scale_weight = attn_weight[:, inner_width:]

    def one_turn(turn_index, state_pair):
        hidden, latent = state_pair
        anchor = (section - turn_index) % device_count
        entry_turn = (device_count - anchor) % device_count
        passed = turn_index - entry_turn
        active = (passed >= 0) & (passed < STEPS * device_count)
        step_index = jnp.clip(passed // device_count, 0, STEPS - 1)
        positions = jnp.arange(STEPS + 1)
        noise_level = jnp.sum(jnp.where(positions == step_index, plan, 0)).astype(jnp.float32)
        next_level = jnp.sum(jnp.where(positions == step_index + 1, plan, 0)).astype(jnp.float32)
        features = time_features(noise_level, mod_weight.shape[0])
        modulation = jnp.dot(features[None, :], mod_weight, preferred_element_type=jnp.float32)[0]
        mod_shift = modulation[:model_width]
        mod_scale = modulation[model_width : 2 * model_width]
        mod_gate = modulation[2 * model_width :]
        embedded = jnp.dot(
            latent.astype(jnp.bfloat16), w_embed, preferred_element_type=jnp.float32
        ).astype(jnp.bfloat16)
        incoming = jnp.where(section == 0, embedded, hidden)
        normed = (layer_norm(incoming) * (1.0 + mod_scale) + mod_shift).astype(jnp.bfloat16)
        projected = jnp.dot(normed, attn_weight, preferred_element_type=jnp.float32).astype(
            jnp.bfloat16
        )
        queries = query_units(projected[:, :inner_width])
        image_keys = projected[:, inner_width : 2 * inner_width]
        image_values = projected[:, 2 * inner_width :]
        live_keys = lax.dynamic_index_in_dim(live_text, anchor, 0, keepdims=False)
        context_rows = lax.dynamic_index_in_dim(context, anchor, 1, keepdims=False)
        text_pairs = jnp.dot(
            context_rows, text_scale_weight, preferred_element_type=jnp.float32
        ).astype(jnp.bfloat16)
        joined_keys = jnp.concatenate([image_keys, text_pairs[:, :inner_width]], 0)
        joined_values = jnp.concatenate([image_values, text_pairs[:, inner_width:]], 0)
        got_queries, got_keys, got_values = (
            lax.all_to_all(queries, "seq", split_axis=0, concat_axis=1, tiled=True),
            lax.all_to_all(key_units(joined_keys), "seq", split_axis=0, concat_axis=1, tiled=True),
            lax.all_to_all(
                key_units(joined_values), "seq", split_axis=0, concat_axis=1, tiled=True
            ),
        )
        all_keys = split_joined(got_keys)
        all_values = split_joined(got_values)
        query_heads = got_queries.reshape(unit_here, seq_count * query_rows, head_size)
        scores = (
            jnp.einsum("uqc,ukc->uqk", query_heads, all_keys, preferred_element_type=jnp.float32)
            * factor
        )
        key_mask = jnp.concatenate([jnp.ones((seq_count * tokens_here,), dtype=bool), live_keys])
        scores = jnp.where(key_mask[None, None, :], scores, -1e30)
        highest = jnp.max(scores, axis=-1, keepdims=True)
        exponents = jnp.exp(scores - highest)
        totals = jnp.sum(exponents, axis=-1, keepdims=True)
        weights = (exponents / totals).astype(jnp.bfloat16)
        attended = jnp.einsum(
            "uqk,ukc->uqc", weights, all_values, preferred_element_type=jnp.float32
        ).astype(jnp.bfloat16)
        returned = lax.all_to_all(
            attended.reshape(unit_here, seq_count * query_rows * head_size),
            "seq",
            split_axis=1,
            concat_axis=0,
            tiled=True,
        )
        merged_heads = from_units(returned)
        update = jnp.dot(merged_heads, proj_weight, preferred_element_type=jnp.float32)
        updated = (incoming.astype(jnp.float32) + mod_gate * update).astype(jnp.bfloat16)
        normed_out = layer_norm(updated).astype(jnp.bfloat16)
        velocity = jnp.dot(normed_out, w_final, preferred_element_type=jnp.float32)
        stepped = latent + (next_level - noise_level) / 1000.0 * velocity
        new_latent = jnp.where(active & (section == device_count - 1), stepped, latent)
        new_hidden = jnp.where(active, updated, hidden)
        sent_hidden, sent_latent = (
            shifted(new_hidden.astype(jnp.float32).astype(jnp.bfloat16), "pipe", 1).astype(
                jnp.float32
            ),
            shifted(new_latent.astype(jnp.bfloat16), "pipe", 1).astype(new_latent.dtype),
        )
        return (sent_hidden.astype(jnp.bfloat16), sent_latent)

    start_hidden = jnp.zeros((tokens_here, model_width), jnp.bfloat16)
    final_pair = lax.fori_loop(
        0, device_count * (STEPS + 1), one_turn, (start_hidden, latent_noise[0, 0])
    )
    return final_pair[1].reshape(latent_noise.shape)


def solution(mesh):
    placed = (
        P("pipe", "batch", "seq", None),
        P(None, "batch", None, "seq"),
        P(None, "batch"),
        P(),
        P("seq", None),
        P(),
        P("pipe", "batch", None),
        P("pipe", "batch", None),
        P("pipe", "batch", None),
        P(),
    )
    return jax.shard_map(
        on_device,
        mesh=mesh,
        in_specs=placed,
        out_specs=P("pipe", "batch", "seq", None),
        check_vma=False,
    )
```

profile of v0, /device:TPU:8, one launch (start us, length us, event | category | flops | bytes accessed | tf_op | source)
XLA Modules:
  0.0 1279.3 jit_solution(2273198371216502025)
XLA Ops:
  12.4 8.0 copy.42
  21.8 181.0 %all-reduce.3 = bf16[256,4,1536]{2,1,0:T(4,128)(2,1)S(1)} all-reduce(f32[256,4,1536]{2,1,0:T(4,128)} %copy.42), channel_id=2, replica_groups=mesh['pipe'=4,'seq'=32,'batch'=2] {'seq'}, use_global_device_ids=true, to_apply=%region_0.0.clone | all-reduce | flops 1572864 | bytes 9437184
  203.0 8.1 slice.137
  211.2 1061.0 %while.17 = (s32[]{:T(128)}, bf16[16,1536]{1,0:T(8,128)(2,1)S(1)}, f32[16,64]{1,0:T(8,128)S(1)}, s32[]{:T(128)}, pred[]{:T(512)}, /*index=5*/bf16[64,1536]{1,0:T...) while((s32[]{:T(128)}, bf16[16,1536]{1,0:T(8,128)(2,1)S(1)}, ...), condition=%wide.region_10.11_spmd, body=%wide.region_1.10_spmd.sunk | while | flops 464863840 | bytes 43831728 | solution.py:185
  224.6 9.6 all-to-all-start
  242.9 9.4 all-to-all-start.1
  286.4 8.1 all-to-all-done.3
  330.6 9.4 all-to-all-start.1
  374.1 8.1 all-to-all-done.3
  418.7 9.4 all-to-all-start.1
  462.2 8.1 all-to-all-done.3
  506.4 9.4 all-to-all-start.1
  549.9 8.1 all-to-all-done.3
  594.6 9.4 all-to-all-start.1
  638.2 8.1 all-to-all-done.3
  682.4 9.4 all-to-all-start.1
  708.0 7.2 all-to-all-done.2
  725.9 8.1 all-to-all-done.3
  770.7 9.4 all-to-all-start.1
  814.3 8.1 all-to-all-done.3
  858.4 9.4 all-to-all-start.1
  902.0 8.1 all-to-all-done.3
  946.7 9.4 all-to-all-start.1
  972.8 7.2 all-to-all-done.2
  990.8 8.1 all-to-all-done.3
  1035.0 9.4 all-to-all-start.1
  1060.6 7.2 all-to-all-done.2
  1078.5 8.1 all-to-all-done.3
  1123.2 9.4 all-to-all-start.1
  1166.8 8.1 all-to-all-done.3
  1210.9 9.4 all-to-all-start.1
  1254.5 8.1 all-to-all-done.3
  (1001 shorter events, 808.1 us)
Async XLA Ops:
  6.5 196.4 %all-gather.6.cloned.1.call-start = ((), (), s32[]{:S(2)}) async-start(), calls=%async_computation.5 | async-start | bytes 21233664 | tf_op jit(solution)/shard_map/all_gather | solution.py:53
  7.3 203.9 %all-gather.4.cloned.1.call-start = ((), (), s32[]{:S(2)}) async-start(), calls=%async_computation.4 | async-start | bytes 3538944 | tf_op jit(solution)/shard_map/all_gather | solution.py:55
  8.0 203.1 %all-gather.8.cloned.1.call-start = ((), (), s32[]{:S(2)}) async-start(), calls=%async_computation.6 | async-start | bytes 7077888 | tf_op jit(solution)/shard_map/all_gather | solution.py:54
  224.6 18.3 %all-to-all-start = ((bf16[32,2,384]{2,1,0:T(2,128)(2,1)}), bf16[32,2,384]{2,1,0:T(2,128)(2,1)S(1)}, u32[]{:S(2)}, u32[]{:S(2)}) async-start(bf16[32,2,384]{2,1,0:T(2,128)(2,1)} %reshape.315), calls=%async_computation | async-start | bytes 98304 | tf_op jit(solution)/shard_map/while/body/eval_jaxpr/all_to_all | solution.py:139
  242.9 18.3 %all-to-all-start.1 = ((bf16[32,2,1152]{2,1,0:T(2,128)(2,1)}), bf16[32,2,1152]{2,1,0:T(2,128)(2,1)S(1)}, u32[]{:S(2)}, u32[]{:S(2)}) async-start(bf16[32,2,1152]{2,1,0:T(2,128)(2,1)} %reshape.319), calls=%async_computation.1 | async-start | bytes 294912 | tf_op jit(solution)/shard_map/while/body/eval_jaxpr/all_to_all | solution.py:140
  261.2 14.5 %all-to-all-start.2 = ((bf16[32,2,1152]{2,1,0:T(2,128)(2,1)}), bf16[32,2,1152]{2,1,0:T(2,128)(2,1)S(1)}, u32[]{:S(2)}, u32[]{:S(2)}) async-start(bf16[32,2,1152]{2,1,0:T(2,128)(2,1)} %reshape.323), calls=%async_computation.2 | async-start | bytes 294912 | tf_op jit(solution)/shard_map/while/body/eval_jaxpr/all_to_all | solution.py:141
  280.3 14.3 %all-to-all-start.3 = ((bf16[32,2,384]{2,1,0:T(2,128)(2,1)}), bf16[32,2,384]{2,1,0:T(2,128)(2,1)S(1)}, u32[]{:S(2)}, u32[]{:S(2)}) async-start(bf16[32,2,384]{2,1,0:T(2,128)(2,1)} %reshape.326), calls=%async_computation.3 | async-start | bytes 98304 | tf_op jit(solution)/shard_map/while/body/eval_jaxpr/all_to_all | solution.py:161
  330.6 18.3 %all-to-all-start.1 = ((bf16[32,2,1152]{2,1,0:T(2,128)(2,1)}), bf16[32,2,1152]{2,1,0:T(2,128)(2,1)S(1)}, u32[]{:S(2)}, u32[]{:S(2)}) async-start(bf16[32,2,1152]{2,1,0:T(2,128)(2,1)} %reshape.319), calls=%async_computation.1 | async-start | bytes 294912 | tf_op jit(solution)/shard_map/while/body/eval_jaxpr/all_to_all | solution.py:140
  348.9 14.5 %all-to-all-start.2 = ((bf16[32,2,1152]{2,1,0:T(2,128)(2,1)}), bf16[32,2,1152]{2,1,0:T(2,128)(2,1)S(1)}, u32[]{:S(2)}, u32[]{:S(2)}) async-start(bf16[32,2,1152]{2,1,0:T(2,128)(2,1)} %reshape.323), calls=%async_computation.2 | async-start | bytes 294912 | tf_op jit(solution)/shard_map/while/body/eval_jaxpr/all_to_all | solution.py:141
  418.7 18.3 %all-to-all-start.1 = ((bf16[32,2,1152]{2,1,0:T(2,128)(2,1)}), bf16[32,2,1152]{2,1,0:T(2,128)(2,1)S(1)}, u32[]{:S(2)}, u32[]{:S(2)}) async-start(bf16[32,2,1152]{2,1,0:T(2,128)(2,1)} %reshape.319), calls=%async_computation.1 | async-start | bytes 294912 | tf_op jit(solution)/shard_map/while/body/eval_jaxpr/all_to_all | solution.py:140
  437.0 14.5 %all-to-all-start.2 = ((bf16[32,2,1152]{2,1,0:T(2,128)(2,1)}), bf16[32,2,1152]{2,1,0:T(2,128)(2,1)S(1)}, u32[]{:S(2)}, u32[]{:S(2)}) async-start(bf16[32,2,1152]{2,1,0:T(2,128)(2,1)} %reshape.323), calls=%async_computation.2 | async-start | bytes 294912 | tf_op jit(solution)/shard_map/while/body/eval_jaxpr/all_to_all | solution.py:141
  456.0 14.3 %all-to-all-start.3 = ((bf16[32,2,384]{2,1,0:T(2,128)(2,1)}), bf16[32,2,384]{2,1,0:T(2,128)(2,1)S(1)}, u32[]{:S(2)}, u32[]{:S(2)}) async-start(bf16[32,2,384]{2,1,0:T(2,128)(2,1)} %reshape.326), calls=%async_computation.3 | async-start | bytes 98304 | tf_op jit(solution)/shard_map/while/body/eval_jaxpr/all_to_all | solution.py:161
  506.4 18.3 %all-to-all-start.1 = ((bf16[32,2,1152]{2,1,0:T(2,128)(2,1)}), bf16[32,2,1152]{2,1,0:T(2,128)(2,1)S(1)}, u32[]{:S(2)}, u32[]{:S(2)}) async-start(bf16[32,2,1152]{2,1,0:T(2,128)(2,1)} %reshape.319), calls=%async_computation.1 | async-start | bytes 294912 | tf_op jit(solution)/shard_map/while/body/eval_jaxpr/all_to_all | solution.py:140
  524.7 14.5 %all-to-all-start.2 = ((bf16[32,2,1152]{2,1,0:T(2,128)(2,1)}), bf16[32,2,1152]{2,1,0:T(2,128)(2,1)S(1)}, u32[]{:S(2)}, u32[]{:S(2)}) async-start(bf16[32,2,1152]{2,1,0:T(2,128)(2,1)} %reshape.323), calls=%async_computation.2 | async-start | bytes 294912 | tf_op jit(solution)/shard_map/while/body/eval_jaxpr/all_to_all | solution.py:141
  543.8 14.3 %all-to-all-start.3 = ((bf16[32,2,384]{2,1,0:T(2,128)(2,1)}), bf16[32,2,384]{2,1,0:T(2,128)(2,1)S(1)}, u32[]{:S(2)}, u32[]{:S(2)}) async-start(bf16[32,2,384]{2,1,0:T(2,128)(2,1)} %reshape.326), calls=%async_computation.3 | async-start | bytes 98304 | tf_op jit(solution)/shard_map/while/body/eval_jaxpr/all_to_all | solution.py:161
  594.6 18.3 %all-to-all-start.1 = ((bf16[32,2,1152]{2,1,0:T(2,128)(2,1)}), bf16[32,2,1152]{2,1,0:T(2,128)(2,1)S(1)}, u32[]{:S(2)}, u32[]{:S(2)}) async-start(bf16[32,2,1152]{2,1,0:T(2,128)(2,1)} %reshape.319), calls=%async_computation.1 | async-start | bytes 294912 | tf_op jit(solution)/shard_map/while/body/eval_jaxpr/all_to_all | solution.py:140
  613.0 14.5 %all-to-all-start.2 = ((bf16[32,2,1152]{2,1,0:T(2,128)(2,1)}), bf16[32,2,1152]{2,1,0:T(2,128)(2,1)S(1)}, u32[]{:S(2)}, u32[]{:S(2)}) async-start(bf16[32,2,1152]{2,1,0:T(2,128)(2,1)} %reshape.323), calls=%async_computation.2 | async-start | bytes 294912 | tf_op jit(solution)/shard_map/while/body/eval_jaxpr/all_to_all | solution.py:141
  632.0 14.3 %all-to-all-start.3 = ((bf16[32,2,384]{2,1,0:T(2,128)(2,1)}), bf16[32,2,384]{2,1,0:T(2,128)(2,1)S(1)}, u32[]{:S(2)}, u32[]{:S(2)}) async-start(bf16[32,2,384]{2,1,0:T(2,128)(2,1)} %reshape.326), calls=%async_computation.3 | async-start | bytes 98304 | tf_op jit(solution)/shard_map/while/body/eval_jaxpr/all_to_all | solution.py:161
  682.4 18.3 %all-to-all-start.1 = ((bf16[32,2,1152]{2,1,0:T(2,128)(2,1)}), bf16[32,2,1152]{2,1,0:T(2,128)(2,1)S(1)}, u32[]{:S(2)}, u32[]{:S(2)}) async-start(bf16[32,2,1152]{2,1,0:T(2,128)(2,1)} %reshape.319), calls=%async_computation.1 | async-start | bytes 294912 | tf_op jit(solution)/shard_map/while/body/eval_jaxpr/all_to_all | solution.py:140
  700.7 14.5 %all-to-all-start.2 = ((bf16[32,2,1152]{2,1,0:T(2,128)(2,1)}), bf16[32,2,1152]{2,1,0:T(2,128)(2,1)S(1)}, u32[]{:S(2)}, u32[]{:S(2)}) async-start(bf16[32,2,1152]{2,1,0:T(2,128)(2,1)} %reshape.323), calls=%async_computation.2 | async-start | bytes 294912 | tf_op jit(solution)/shard_map/while/body/eval_jaxpr/all_to_all | solution.py:141
  770.7 18.3 %all-to-all-start.1 = ((bf16[32,2,1152]{2,1,0:T(2,128)(2,1)}), bf16[32,2,1152]{2,1,0:T(2,128)(2,1)S(1)}, u32[]{:S(2)}, u32[]{:S(2)}) async-start(bf16[32,2,1152]{2,1,0:T(2,128)(2,1)} %reshape.319), calls=%async_computation.1 | async-start | bytes 294912 | tf_op jit(solution)/shard_map/while/body/eval_jaxpr/all_to_all | solution.py:140
  789.1 14.5 %all-to-all-start.2 = ((bf16[32,2,1152]{2,1,0:T(2,128)(2,1)}), bf16[32,2,1152]{2,1,0:T(2,128)(2,1)S(1)}, u32[]{:S(2)}, u32[]{:S(2)}) async-start(bf16[32,2,1152]{2,1,0:T(2,128)(2,1)} %reshape.323), calls=%async_computation.2 | async-start | bytes 294912 | tf_op jit(solution)/shard_map/while/body/eval_jaxpr/all_to_all | solution.py:141
  858.4 18.3 %all-to-all-start.1 = ((bf16[32,2,1152]{2,1,0:T(2,128)(2,1)}), bf16[32,2,1152]{2,1,0:T(2,128)(2,1)S(1)}, u32[]{:S(2)}, u32[]{:S(2)}) async-start(bf16[32,2,1152]{2,1,0:T(2,128)(2,1)} %reshape.319), calls=%async_computation.1 | async-start | bytes 294912 | tf_op jit(solution)/shard_map/while/body/eval_jaxpr/all_to_all | solution.py:140
  876.8 14.5 %all-to-all-start.2 = ((bf16[32,2,1152]{2,1,0:T(2,128)(2,1)}), bf16[32,2,1152]{2,1,0:T(2,128)(2,1)S(1)}, u32[]{:S(2)}, u32[]{:S(2)}) async-start(bf16[32,2,1152]{2,1,0:T(2,128)(2,1)} %reshape.323), calls=%async_computation.2 | async-start | bytes 294912 | tf_op jit(solution)/shard_map/while/body/eval_jaxpr/all_to_all | solution.py:141
  946.7 18.7 %all-to-all-start.1 = ((bf16[32,2,1152]{2,1,0:T(2,128)(2,1)}), bf16[32,2,1152]{2,1,0:T(2,128)(2,1)S(1)}, u32[]{:S(2)}, u32[]{:S(2)}) async-start(bf16[32,2,1152]{2,1,0:T(2,128)(2,1)} %reshape.319), calls=%async_computation.1 | async-start | bytes 294912 | tf_op jit(solution)/shard_map/while/body/eval_jaxpr/all_to_all | solution.py:140
  965.4 14.7 %all-to-all-start.2 = ((bf16[32,2,1152]{2,1,0:T(2,128)(2,1)}), bf16[32,2,1152]{2,1,0:T(2,128)(2,1)S(1)}, u32[]{:S(2)}, u32[]{:S(2)}) async-start(bf16[32,2,1152]{2,1,0:T(2,128)(2,1)} %reshape.323), calls=%async_computation.2 | async-start | bytes 294912 | tf_op jit(solution)/shard_map/while/body/eval_jaxpr/all_to_all | solution.py:141
  1035.0 18.3 %all-to-all-start.1 = ((bf16[32,2,1152]{2,1,0:T(2,128)(2,1)}), bf16[32,2,1152]{2,1,0:T(2,128)(2,1)S(1)}, u32[]{:S(2)}, u32[]{:S(2)}) async-start(bf16[32,2,1152]{2,1,0:T(2,128)(2,1)} %reshape.319), calls=%async_computation.1 | async-start | bytes 294912 | tf_op jit(solution)/shard_map/while/body/eval_jaxpr/all_to_all | solution.py:140
  1053.3 14.5 %all-to-all-start.2 = ((bf16[32,2,1152]{2,1,0:T(2,128)(2,1)}), bf16[32,2,1152]{2,1,0:T(2,128)(2,1)S(1)}, u32[]{:S(2)}, u32[]{:S(2)}) async-start(bf16[32,2,1152]{2,1,0:T(2,128)(2,1)} %reshape.323), calls=%async_computation.2 | async-start | bytes 294912 | tf_op jit(solution)/shard_map/while/body/eval_jaxpr/all_to_all | solution.py:141
  1123.2 18.3 %all-to-all-start.1 = ((bf16[32,2,1152]{2,1,0:T(2,128)(2,1)}), bf16[32,2,1152]{2,1,0:T(2,128)(2,1)S(1)}, u32[]{:S(2)}, u32[]{:S(2)}) async-start(bf16[32,2,1152]{2,1,0:T(2,128)(2,1)} %reshape.319), calls=%async_computation.1 | async-start | bytes 294912 | tf_op jit(solution)/shard_map/while/body/eval_jaxpr/all_to_all | solution.py:140
  1141.5 14.5 %all-to-all-start.2 = ((bf16[32,2,1152]{2,1,0:T(2,128)(2,1)}), bf16[32,2,1152]{2,1,0:T(2,128)(2,1)S(1)}, u32[]{:S(2)}, u32[]{:S(2)}) async-start(bf16[32,2,1152]{2,1,0:T(2,128)(2,1)} %reshape.323), calls=%async_computation.2 | async-start | bytes 294912 | tf_op jit(solution)/shard_map/while/body/eval_jaxpr/all_to_all | solution.py:141
  1210.9 18.3 %all-to-all-start.1 = ((bf16[32,2,1152]{2,1,0:T(2,128)(2,1)}), bf16[32,2,1152]{2,1,0:T(2,128)(2,1)S(1)}, u32[]{:S(2)}, u32[]{:S(2)}) async-start(bf16[32,2,1152]{2,1,0:T(2,128)(2,1)} %reshape.319), calls=%async_computation.1 | async-start | bytes 294912 | tf_op jit(solution)/shard_map/while/body/eval_jaxpr/all_to_all | solution.py:140
  1229.3 14.5 %all-to-all-start.2 = ((bf16[32,2,1152]{2,1,0:T(2,128)(2,1)}), bf16[32,2,1152]{2,1,0:T(2,128)(2,1)S(1)}, u32[]{:S(2)}, u32[]{:S(2)}) async-start(bf16[32,2,1152]{2,1,0:T(2,128)(2,1)} %reshape.323), calls=%async_computation.2 | async-start | bytes 294912 | tf_op jit(solution)/shard_map/while/body/eval_jaxpr/all_to_all | solution.py:141
  (52 other events, 620.0 us)
Sparse Core Ops, SparseCore 0:
  9.2 34.6 all-gather.5
  45.7 17.5 all-gather.3
  65.1 21.0 all-gather.7
where the time goes:
time: 1280 us
  starting transfers between devices  331 us (26%)
  waiting for transfers between devices  301 us (24%)
  matrix products  225 us (18%)
  blocking collectives  181 us (14%)
  local copies, waits for them, and re-layouts  112 us (9%)
  other arithmetic  97.6 us (8%)
  loops' own time  18.3 us (1%)
  between operations  13.9 us (1%)
    unnamed x1, blocking collectives  181 us
    all_to_all x12, starting transfers between devices, one_turn(): lax.all_to_all(key_units(joined_keys), 'seq', split_axis=0, concat_axis=1...  113 us
    all_to_all x12, waiting for transfers between devices, one_turn(): lax.all_to_all(attended.reshape(unit_here, seq_count * query_rows * head_...  97.6 us
    all_to_all x12, waiting for transfers between devices, one_turn(): lax.all_to_all(key_units(joined_values), 'seq', split_axis=0, concat_axis...  86.2 us
    dot_general x12, matrix products, one_turn(): jnp.dot(normed, attn_weight, preferred_element_type=jnp.float32)  84.3 us
    all_to_all x12, waiting for transfers between devices, one_turn(): lax.all_to_all(key_units(joined_keys), 'seq', split_axis=0, concat_axis=1...  68.3 us
    all_to_all x12, starting transfers between devices, one_turn(): lax.all_to_all(attended.reshape(unit_here, seq_count * query_rows * head_...  66.6 us
    all_to_all x12, starting transfers between devices, one_turn(): lax.all_to_all(key_units(joined_values), 'seq', split_axis=0, concat_axis...  65.9 us
  transfers between devices with their start and end apart: 75, of which 60 were waited for; matrix products, arithmetic and copies ran while one was open for 14% of the time, Pallas kernels for 0%

commit v1 on v0

--- a/solution.py
+++ b/solution.py
@@ -7,6 +7,13 @@
 HEADS = 16
 STEPS = 2
 epsilon = 1e-06
+
+
+def extend_loads(u_in):
+    return jnp.concatenate(
+        jax.lax.all_to_all(jnp.stack(jnp.split(u_in, jax.lax.axis_size("seq"), 1), 0), "seq", 0, 0),
+        0,
+    )
 
 
 def shifted(value, axis, by):
@@ -158,13 +165,7 @@
         attended = jnp.einsum(
             "uqk,ukc->uqc", weights, all_values, preferred_element_type=jnp.float32
         ).astype(jnp.bfloat16)
-        returned = lax.all_to_all(
-            attended.reshape(unit_here, seq_count * query_rows * head_size),
-            "seq",
-            split_axis=1,
-            concat_axis=0,
-            tiled=True,
-        )
+        returned = extend_loads(attended.reshape(unit_here, seq_count * query_rows * head_size))
         merged_heads = from_units(returned)
         update = jnp.dot(merged_heads, proj_weight, preferred_element_type=jnp.float32)
         updated = (incoming.astype(jnp.float32) + mod_gate * update).astype(jnp.bfloat16)

time: 1280 us -> 1290 us (level)
    while x108 -> x468, local copies, waits for them, and re-layouts: 41.6 us -> 39.4 us
where the time goes in v1:
time: 1290 us
  starting transfers between devices  331 us (26%)
  waiting for transfers between devices  301 us (23%)
  matrix products  225 us (17%)
  blocking collectives  181 us (14%)
  local copies, waits for them, and re-layouts  114 us (9%)
  other arithmetic  101 us (8%)
  loops' own time  19.6 us (2%)
  between operations  13.9 us (1%)
    unnamed x1, blocking collectives  181 us
    all_to_all x12, starting transfers between devices, one_turn(): lax.all_to_all(key_units(joined_keys), 'seq', split_axis=0, concat_axis=1...  113 us
    all_to_all x12, waiting for transfers between devices, extend_loads(): jax.lax.all_to_all(jnp.stack(jnp.split(u_in, jax.lax.axis_size('seq'), 1)...  97.7 us
    all_to_all x12, waiting for transfers between devices, one_turn(): lax.all_to_all(key_units(joined_values), 'seq', split_axis=0, concat_axis...  86.2 us
    dot_general x12, matrix products, one_turn(): jnp.dot(normed, attn_weight, preferred_element_type=jnp.float32)  84.3 us
    all_to_all x12, waiting for transfers between devices, one_turn(): lax.all_to_all(key_units(joined_keys), 'seq', split_axis=0, concat_axis=1...  68.2 us
    all_to_all x12, starting transfers between devices, extend_loads(): jax.lax.all_to_all(jnp.stack(jnp.split(u_in, jax.lax.axis_size('seq'), 1)...  66.5 us
    all_to_all x12, starting transfers between devices, one_turn(): lax.all_to_all(key_units(joined_values), 'seq', split_axis=0, concat_axis...  65.9 us
  transfers between devices with their start and end apart: 75, of which 60 were waited for; matrix products, arithmetic and copies ran while one was open for 14% of the time, Pallas kernels for 0%

profile of v1, /device:TPU:8, one launch (start us, length us, event | category | flops | bytes accessed | tf_op | source)
XLA Modules:
  0.0 1286.0 jit_solution(8186045856491485714)
XLA Ops:
  12.4 8.0 copy.40
  21.8 181.4 %all-reduce.3 = bf16[256,4,1536]{2,1,0:T(4,128)(2,1)} all-reduce(f32[256,4,1536]{2,1,0:T(4,128)} %copy.40), channel_id=2, replica_groups=mesh['pipe'=4,'seq'=32,'batch'=2] {'seq'}, use_global_device_ids=true, to_apply=%region_0.0.clone | all-reduce | flops 1572864 | bytes 9437184
  204.3 8.1 slice.137
  212.5 1066.4 %while.17 = (s32[]{:T(128)}, bf16[16,1536]{1,0:T(8,128)(2,1)S(1)}, f32[16,64]{1,0:T(8,128)S(1)}, s32[]{:T(128)}, pred[]{:T(512)}, /*index=5*/bf16[64,1536]{1,0:T...) while((s32[]{:T(128)}, bf16[16,1536]{1,0:T(8,128)(2,1)S(1)}, ...), condition=%wide.region_10.11_spmd, body=%wide.region_1.10_spmd.sunk | while | flops 464863840 | bytes 44026800 | solution.py:186
  225.9 9.6 all-to-all-start
  244.2 9.4 all-to-all-start.1
  288.1 8.1 all-to-all-done.3
  332.3 9.4 all-to-all-start.1
  376.3 8.1 all-to-all-done.3
  421.0 9.4 all-to-all-start.1
  464.9 8.1 all-to-all-done.3
  509.1 9.4 all-to-all-start.1
  553.1 8.1 all-to-all-done.3
  597.7 9.4 all-to-all-start.1
  641.7 8.1 all-to-all-done.3
  685.9 9.4 all-to-all-start.1
  711.5 7.2 all-to-all-done.2
  729.9 8.2 all-to-all-done.3
  774.8 9.4 all-to-all-start.1
  818.9 8.1 all-to-all-done.3
  863.0 9.4 all-to-all-start.1
  907.0 8.1 all-to-all-done.3
  951.5 9.4 all-to-all-start.1
  977.7 7.2 all-to-all-done.2
  996.1 8.1 all-to-all-done.3
  1040.3 9.4 all-to-all-start.1
  1066.0 7.2 all-to-all-done.2
  1084.3 8.1 all-to-all-done.3
  1129.0 9.4 all-to-all-start.1
  1173.0 8.1 all-to-all-done.3
  1217.2 9.4 all-to-all-start.1
  1261.2 8.1 all-to-all-done.3
  (1385 shorter events, 813.1 us)
Async XLA Ops:
  6.5 197.7 %all-gather.6.cloned.1.call-start = ((), (), s32[]{:S(2)}) async-start(), calls=%async_computation.5 | async-start | bytes 21233664 | tf_op jit(solution)/shard_map/all_gather | solution.py:60
  7.3 205.2 %all-gather.4.cloned.1.call-start = ((), (), s32[]{:S(2)}) async-start(), calls=%async_computation.4 | async-start | bytes 3538944 | tf_op jit(solution)/shard_map/all_gather | solution.py:62
  8.0 204.4 %all-gather.8.cloned.1.call-start = ((), (), s32[]{:S(2)}) async-start(), calls=%async_computation.6 | async-start | bytes 7077888 | tf_op jit(solution)/shard_map/all_gather | solution.py:61
  225.9 18.3 %all-to-all-start = ((bf16[32,2,384]{2,1,0:T(2,128)(2,1)}), bf16[32,2,384]{2,1,0:T(2,128)(2,1)S(1)}, u32[]{:S(2)}, u32[]{:S(2)}) async-start(bf16[32,2,384]{2,1,0:T(2,128)(2,1)} %reshape.310), calls=%async_computation | async-start | bytes 98304 | tf_op jit(solution)/shard_map/while/body/eval_jaxpr/all_to_all | solution.py:146
  244.2 18.3 %all-to-all-start.1 = ((bf16[32,2,1152]{2,1,0:T(2,128)(2,1)}), bf16[32,2,1152]{2,1,0:T(2,128)(2,1)S(1)}, u32[]{:S(2)}, u32[]{:S(2)}) async-start(bf16[32,2,1152]{2,1,0:T(2,128)(2,1)} %reshape.314), calls=%async_computation.1 | async-start | bytes 294912 | tf_op jit(solution)/shard_map/while/body/eval_jaxpr/all_to_all | solution.py:147
  262.5 14.5 %all-to-all-start.2 = ((bf16[32,2,1152]{2,1,0:T(2,128)(2,1)}), bf16[32,2,1152]{2,1,0:T(2,128)(2,1)S(1)}, u32[]{:S(2)}, u32[]{:S(2)}) async-start(bf16[32,2,1152]{2,1,0:T(2,128)(2,1)} %reshape.318), calls=%async_computation.2 | async-start | bytes 294912 | tf_op jit(solution)/shard_map/while/body/eval_jaxpr/all_to_all | solution.py:148
  332.3 18.3 %all-to-all-start.1 = ((bf16[32,2,1152]{2,1,0:T(2,128)(2,1)}), bf16[32,2,1152]{2,1,0:T(2,128)(2,1)S(1)}, u32[]{:S(2)}, u32[]{:S(2)}) async-start(bf16[32,2,1152]{2,1,0:T(2,128)(2,1)} %reshape.314), calls=%async_computation.1 | async-start | bytes 294912 | tf_op jit(solution)/shard_map/while/body/eval_jaxpr/all_to_all | solution.py:147
  350.7 14.5 %all-to-all-start.2 = ((bf16[32,2,1152]{2,1,0:T(2,128)(2,1)}), bf16[32,2,1152]{2,1,0:T(2,128)(2,1)S(1)}, u32[]{:S(2)}, u32[]{:S(2)}) async-start(bf16[32,2,1152]{2,1,0:T(2,128)(2,1)} %reshape.318), calls=%async_computation.2 | async-start | bytes 294912 | tf_op jit(solution)/shard_map/while/body/eval_jaxpr/all_to_all | solution.py:148
  421.0 18.3 %all-to-all-start.1 = ((bf16[32,2,1152]{2,1,0:T(2,128)(2,1)}), bf16[32,2,1152]{2,1,0:T(2,128)(2,1)S(1)}, u32[]{:S(2)}, u32[]{:S(2)}) async-start(bf16[32,2,1152]{2,1,0:T(2,128)(2,1)} %reshape.314), calls=%async_computation.1 | async-start | bytes 294912 | tf_op jit(solution)/shard_map/while/body/eval_jaxpr/all_to_all | solution.py:147
  439.3 14.4 %all-to-all-start.2 = ((bf16[32,2,1152]{2,1,0:T(2,128)(2,1)}), bf16[32,2,1152]{2,1,0:T(2,128)(2,1)S(1)}, u32[]{:S(2)}, u32[]{:S(2)}) async-start(bf16[32,2,1152]{2,1,0:T(2,128)(2,1)} %reshape.318), calls=%async_computation.2 | async-start | bytes 294912 | tf_op jit(solution)/shard_map/while/body/eval_jaxpr/all_to_all | solution.py:148
  509.1 18.3 %all-to-all-start.1 = ((bf16[32,2,1152]{2,1,0:T(2,128)(2,1)}), bf16[32,2,1152]{2,1,0:T(2,128)(2,1)S(1)}, u32[]{:S(2)}, u32[]{:S(2)}) async-start(bf16[32,2,1152]{2,1,0:T(2,128)(2,1)} %reshape.314), calls=%async_computation.1 | async-start | bytes 294912 | tf_op jit(solution)/shard_map/while/body/eval_jaxpr/all_to_all | solution.py:147
  527.4 14.5 %all-to-all-start.2 = ((bf16[32,2,1152]{2,1,0:T(2,128)(2,1)}), bf16[32,2,1152]{2,1,0:T(2,128)(2,1)S(1)}, u32[]{:S(2)}, u32[]{:S(2)}) async-start(bf16[32,2,1152]{2,1,0:T(2,128)(2,1)} %reshape.318), calls=%async_computation.2 | async-start | bytes 294912 | tf_op jit(solution)/shard_map/while/body/eval_jaxpr/all_to_all | solution.py:148
  546.9 14.3 %all-to-all-start.3 = ((bf16[32,2,384]{2,1,0:T(2,128)(2,1)}), bf16[32,2,384]{2,1,0:T(2,128)(2,1)S(1)}, u32[]{:S(2)}, u32[]{:S(2)}) async-start(bf16[32,2,384]{2,1,0:T(2,128)(2,1)} %reshape.322), calls=%async_computation.3 | async-start | bytes 98304 | tf_op jit(solution)/shard_map/while/body/eval_jaxpr/all_to_all | solution.py:14
  597.7 18.3 %all-to-all-start.1 = ((bf16[32,2,1152]{2,1,0:T(2,128)(2,1)}), bf16[32,2,1152]{2,1,0:T(2,128)(2,1)S(1)}, u32[]{:S(2)}, u32[]{:S(2)}) async-start(bf16[32,2,1152]{2,1,0:T(2,128)(2,1)} %reshape.314), calls=%async_computation.1 | async-start | bytes 294912 | tf_op jit(solution)/shard_map/while/body/eval_jaxpr/all_to_all | solution.py:147
  616.0 14.5 %all-to-all-start.2 = ((bf16[32,2,1152]{2,1,0:T(2,128)(2,1)}), bf16[32,2,1152]{2,1,0:T(2,128)(2,1)S(1)}, u32[]{:S(2)}, u32[]{:S(2)}) async-start(bf16[32,2,1152]{2,1,0:T(2,128)(2,1)} %reshape.318), calls=%async_computation.2 | async-start | bytes 294912 | tf_op jit(solution)/shard_map/while/body/eval_jaxpr/all_to_all | solution.py:148
  635.6 14.3 %all-to-all-start.3 = ((bf16[32,2,384]{2,1,0:T(2,128)(2,1)}), bf16[32,2,384]{2,1,0:T(2,128)(2,1)S(1)}, u32[]{:S(2)}, u32[]{:S(2)}) async-start(bf16[32,2,384]{2,1,0:T(2,128)(2,1)} %reshape.322), calls=%async_computation.3 | async-start | bytes 98304 | tf_op jit(solution)/shard_map/while/body/eval_jaxpr/all_to_all | solution.py:14
  685.9 18.3 %all-to-all-start.1 = ((bf16[32,2,1152]{2,1,0:T(2,128)(2,1)}), bf16[32,2,1152]{2,1,0:T(2,128)(2,1)S(1)}, u32[]{:S(2)}, u32[]{:S(2)}) async-start(bf16[32,2,1152]{2,1,0:T(2,128)(2,1)} %reshape.314), calls=%async_computation.1 | async-start | bytes 294912 | tf_op jit(solution)/shard_map/while/body/eval_jaxpr/all_to_all | solution.py:147
  704.3 14.5 %all-to-all-start.2 = ((bf16[32,2,1152]{2,1,0:T(2,128)(2,1)}), bf16[32,2,1152]{2,1,0:T(2,128)(2,1)S(1)}, u32[]{:S(2)}, u32[]{:S(2)}) async-start(bf16[32,2,1152]{2,1,0:T(2,128)(2,1)} %reshape.318), calls=%async_computation.2 | async-start | bytes 294912 | tf_op jit(solution)/shard_map/while/body/eval_jaxpr/all_to_all | solution.py:148
  723.8 14.3 %all-to-all-start.3 = ((bf16[32,2,384]{2,1,0:T(2,128)(2,1)}), bf16[32,2,384]{2,1,0:T(2,128)(2,1)S(1)}, u32[]{:S(2)}, u32[]{:S(2)}) async-start(bf16[32,2,384]{2,1,0:T(2,128)(2,1)} %reshape.322), calls=%async_computation.3 | async-start | bytes 98304 | tf_op jit(solution)/shard_map/while/body/eval_jaxpr/all_to_all | solution.py:14
  774.8 18.3 %all-to-all-start.1 = ((bf16[32,2,1152]{2,1,0:T(2,128)(2,1)}), bf16[32,2,1152]{2,1,0:T(2,128)(2,1)S(1)}, u32[]{:S(2)}, u32[]{:S(2)}) async-start(bf16[32,2,1152]{2,1,0:T(2,128)(2,1)} %reshape.314), calls=%async_computation.1 | async-start | bytes 294912 | tf_op jit(solution)/shard_map/while/body/eval_jaxpr/all_to_all | solution.py:147
  793.2 14.5 %all-to-all-start.2 = ((bf16[32,2,1152]{2,1,0:T(2,128)(2,1)}), bf16[32,2,1152]{2,1,0:T(2,128)(2,1)S(1)}, u32[]{:S(2)}, u32[]{:S(2)}) async-start(bf16[32,2,1152]{2,1,0:T(2,128)(2,1)} %reshape.318), calls=%async_computation.2 | async-start | bytes 294912 | tf_op jit(solution)/shard_map/while/body/eval_jaxpr/all_to_all | solution.py:148
  863.0 18.3 %all-to-all-start.1 = ((bf16[32,2,1152]{2,1,0:T(2,128)(2,1)}), bf16[32,2,1152]{2,1,0:T(2,128)(2,1)S(1)}, u32[]{:S(2)}, u32[]{:S(2)}) async-start(bf16[32,2,1152]{2,1,0:T(2,128)(2,1)} %reshape.314), calls=%async_computation.1 | async-start | bytes 294912 | tf_op jit(solution)/shard_map/while/body/eval_jaxpr/all_to_all | solution.py:147
  881.4 14.5 %all-to-all-start.2 = ((bf16[32,2,1152]{2,1,0:T(2,128)(2,1)}), bf16[32,2,1152]{2,1,0:T(2,128)(2,1)S(1)}, u32[]{:S(2)}, u32[]{:S(2)}) async-start(bf16[32,2,1152]{2,1,0:T(2,128)(2,1)} %reshape.318), calls=%async_computation.2 | async-start | bytes 294912 | tf_op jit(solution)/shard_map/while/body/eval_jaxpr/all_to_all | solution.py:148
  951.5 18.5 %all-to-all-start.1 = ((bf16[32,2,1152]{2,1,0:T(2,128)(2,1)}), bf16[32,2,1152]{2,1,0:T(2,128)(2,1)S(1)}, u32[]{:S(2)}, u32[]{:S(2)}) async-start(bf16[32,2,1152]{2,1,0:T(2,128)(2,1)} %reshape.314), calls=%async_computation.1 | async-start | bytes 294912 | tf_op jit(solution)/shard_map/while/body/eval_jaxpr/all_to_all | solution.py:147
  970.1 14.8 %all-to-all-start.2 = ((bf16[32,2,1152]{2,1,0:T(2,128)(2,1)}), bf16[32,2,1152]{2,1,0:T(2,128)(2,1)S(1)}, u32[]{:S(2)}, u32[]{:S(2)}) async-start(bf16[32,2,1152]{2,1,0:T(2,128)(2,1)} %reshape.318), calls=%async_computation.2 | async-start | bytes 294912 | tf_op jit(solution)/shard_map/while/body/eval_jaxpr/all_to_all | solution.py:148
  1040.3 18.3 %all-to-all-start.1 = ((bf16[32,2,1152]{2,1,0:T(2,128)(2,1)}), bf16[32,2,1152]{2,1,0:T(2,128)(2,1)S(1)}, u32[]{:S(2)}, u32[]{:S(2)}) async-start(bf16[32,2,1152]{2,1,0:T(2,128)(2,1)} %reshape.314), calls=%async_computation.1 | async-start | bytes 294912 | tf_op jit(solution)/shard_map/while/body/eval_jaxpr/all_to_all | solution.py:147
  1058.7 14.5 %all-to-all-start.2 = ((bf16[32,2,1152]{2,1,0:T(2,128)(2,1)}), bf16[32,2,1152]{2,1,0:T(2,128)(2,1)S(1)}, u32[]{:S(2)}, u32[]{:S(2)}) async-start(bf16[32,2,1152]{2,1,0:T(2,128)(2,1)} %reshape.318), calls=%async_computation.2 | async-start | bytes 294912 | tf_op jit(solution)/shard_map/while/body/eval_jaxpr/all_to_all | solution.py:148
  1129.0 18.3 %all-to-all-start.1 = ((bf16[32,2,1152]{2,1,0:T(2,128)(2,1)}), bf16[32,2,1152]{2,1,0:T(2,128)(2,1)S(1)}, u32[]{:S(2)}, u32[]{:S(2)}) async-start(bf16[32,2,1152]{2,1,0:T(2,128)(2,1)} %reshape.314), calls=%async_computation.1 | async-start | bytes 294912 | tf_op jit(solution)/shard_map/while/body/eval_jaxpr/all_to_all | solution.py:147
  1147.3 14.5 %all-to-all-start.2 = ((bf16[32,2,1152]{2,1,0:T(2,128)(2,1)}), bf16[32,2,1152]{2,1,0:T(2,128)(2,1)S(1)}, u32[]{:S(2)}, u32[]{:S(2)}) async-start(bf16[32,2,1152]{2,1,0:T(2,128)(2,1)} %reshape.318), calls=%async_computation.2 | async-start | bytes 294912 | tf_op jit(solution)/shard_map/while/body/eval_jaxpr/all_to_all | solution.py:148
  1217.2 18.3 %all-to-all-start.1 = ((bf16[32,2,1152]{2,1,0:T(2,128)(2,1)}), bf16[32,2,1152]{2,1,0:T(2,128)(2,1)S(1)}, u32[]{:S(2)}, u32[]{:S(2)}) async-start(bf16[32,2,1152]{2,1,0:T(2,128)(2,1)} %reshape.314), calls=%async_computation.1 | async-start | bytes 294912 | tf_op jit(solution)/shard_map/while/body/eval_jaxpr/all_to_all | solution.py:147
  1235.6 14.5 %all-to-all-start.2 = ((bf16[32,2,1152]{2,1,0:T(2,128)(2,1)}), bf16[32,2,1152]{2,1,0:T(2,128)(2,1)S(1)}, u32[]{:S(2)}, u32[]{:S(2)}) async-start(bf16[32,2,1152]{2,1,0:T(2,128)(2,1)} %reshape.318), calls=%async_computation.2 | async-start | bytes 294912 | tf_op jit(solution)/shard_map/while/body/eval_jaxpr/all_to_all | solution.py:148
  1255.1 14.3 %all-to-all-start.3 = ((bf16[32,2,384]{2,1,0:T(2,128)(2,1)}), bf16[32,2,384]{2,1,0:T(2,128)(2,1)S(1)}, u32[]{:S(2)}, u32[]{:S(2)}) async-start(bf16[32,2,384]{2,1,0:T(2,128)(2,1)} %reshape.322), calls=%async_computation.3 | async-start | bytes 98304 | tf_op jit(solution)/shard_map/while/body/eval_jaxpr/all_to_all | solution.py:14
  (52 other events, 621.3 us)
Sparse Core Ops, SparseCore 0:
  9.2 34.6 all-gather.5
  45.7 17.5 all-gather.3
  65.1 21.0 all-gather.7
